TPU v7x, 32 devices: a whole 2x2x4 slice. The times are simulated.
32 devices in a mesh: rep: 4 (over y, x), shard: 8 (over z, core).
Axes of the slice: x: 2, y: 2, z: 4, core: 2. Of those that a mesh axis runs over, the one named last changes fastest.
Arguments:
- slow_weights: float32 [4, 64, 8192], P('rep', 'shard'), may hold values from -0.12 to 0.12
- outer_momentum: float32 [4, 64, 8192], P('rep', 'shard'), may hold values from -0.018 to 0.018
- adam_first: float32 [4, 64, 8192], P('rep', 'shard'), may hold values from -1 to 1
- adam_second: float32 [4, 64, 8192], P('rep', 'shard'), may hold values from 0 to 1, as said below
- gradients: bfloat16 [4, 4, 4, 64, 8192], P(None, None, 'rep', 'shard'), may hold values from -1000 to 1000, as said below
- pair_mask: int32 [4], replicated, may hold values from 1 to 2, as said below
Outputs:
- new_slow: float32 [4, 64, 8192], P('rep', 'shard')
- new_momentum: float32 [4, 64, 8192], P('rep', 'shard')
- new_first: float32 [4, 64, 8192], P('rep', 'shard')
- new_second: float32 [4, 64, 8192], P('rep', 'shard')
Inputs may be any that keep to these rules, and one draw needn't show every extreme that they name: In outer step t replica r is matched with replica r XOR pair_mask[t] (bitwise exclusive or); 4 is a power of two, and every pair_mask[t] is a single power of two. Every bit of 3 occurs in some outer step; in which order is drawn anew. `gradients`: gradients of all inner updates. `adam_second`: second moments, positive.
All inputs are finite; a program needn't handle non-finite values.
Results may differ from a plain program's by a relative error of at most 0.0018.
Values may be sent and summed in bfloat16 or wider, within the bound.
A program may use at most 64 MiB of HBM per device.

v0:
```python
from functools import partial

import jax
import jax.numpy as jnp
from jax import lax
from jax.sharding import PartitionSpec as P

clip_limit = 1.0
beta_one = 0.9
beta_two = 0.95
adam_eps = 1e-08
inner_rate = 0.001
decay_rate = 0.1
outer_rate = 0.7
momentum_rate = 0.9
mix_rate = 0.25


def shortened(value):

    def short(part):
        return part.astype(jnp.bfloat16) if part.dtype == jnp.float32 else part

    return jax.tree.map(short, value)


def swapped(value, axis, stride):
    mask = 2**stride
    pairs = [(source, source ^ mask) for source in range(lax.axis_size(axis))]
    return lax.ppermute(value, axis, pairs)


def swap_partner(bit_index, payload):
    return jax.tree.map(
        lambda part, own: part.astype(own.dtype),
        swapped(shortened(payload), "rep", bit_index),
        payload,
    )


def on_device(slow_weights, outer_momentum, adam_first, adam_second, gradients, pair_mask):
    bit_count = lax.axis_size("rep").bit_length() - 1
    slow_now = slow_weights
    momentum = outer_momentum
    moment_one = adam_first
    moment_two = adam_second
    for outer_step in range(gradients.shape[0]):
        fast_weights = slow_now
        for inner_step in range(gradients.shape[1]):
            gradient = gradients[outer_step, inner_step].astype(jnp.float32)
            square_sum = lax.psum(jnp.sum(gradient * gradient), "shard")
            factor = clip_limit / jnp.maximum(jnp.sqrt(square_sum), clip_limit)
            clipped = factor * gradient
            moment_one = beta_one * moment_one + (1.0 - beta_one) * clipped
            moment_two = beta_two * moment_two + (1.0 - beta_two) * clipped * clipped
            fast_weights = fast_weights - inner_rate * (
                moment_one / (jnp.sqrt(moment_two) + adam_eps) + decay_rate * fast_weights
            )
        pseudo_grad = (slow_now - fast_weights).astype(jnp.bfloat16)
        sent_slow = slow_now.astype(jnp.bfloat16)
        step_mask = pair_mask[outer_step]
        position = jnp.zeros((), jnp.int32)
        for bit_index in range(bit_count):
            position = position + bit_index * jnp.bitwise_and(
                jnp.right_shift(step_mask, bit_index), 1
            )
        branches = [partial(swap_partner, bit_index) for bit_index in range(bit_count)]
        arrived = lax.switch(position, branches, (pseudo_grad, sent_slow))
        other_pseudo = arrived[0].astype(jnp.float32)
        other_slow = arrived[1].astype(jnp.float32)
        average = 0.5 * (pseudo_grad.astype(jnp.float32) + other_pseudo)
        momentum = momentum_rate * momentum + average
        slow_now = (
            slow_now
            + mix_rate * (other_slow - slow_now)
            - outer_rate * (average + momentum_rate * momentum)
        )
    return (slow_now, momentum, moment_one, moment_two)


def solution(mesh):
    return jax.shard_map(
        on_device,
        mesh=mesh,
        in_specs=(
            P("rep", "shard", None),
            P("rep", "shard", None),
            P("rep", "shard", None),
            P("rep", "shard", None),
            P(None, None, "rep", "shard", None),
            P(),
        ),
        out_specs=(
            P("rep", "shard", None),
            P("rep", "shard", None),
            P("rep", "shard", None),
            P("rep", "shard", None),
        ),
        check_vma=False,
    )
```

profile of v0, /device:TPU:0, one launch (start us, length us, event | category | flops | bytes accessed | tf_op | source)
XLA Modules:
  0.0 79.3 jit_solution(13219645757225029382)
XLA Ops:
  0.7 1.5 %fusion.109 = (s32[1]{0:T(128)}, s32[1]{0:T(128)}, s32[1]{0:T(128)}, s32[1]{0:T(128)}) fusion(s32[4]{0:T(128)} %param.19), kind=kLoop, calls=%fused_computation.164 | loop fusion | bytes 32 | tf_op jit(solution)/shard_map/slice | solution.py:61
  4.7 2.8 %fusion.48 = (f32[]{:T(128)}, f32[]{:T(128)}, f32[]{:T(128)}, f32[]{:T(128)}, f32[]{:T(128)}, /*index=5*/f32[]{:T(128)}, f32[]{:T(128)}, f32[]{:T(128)}, f32[]{:...) fusion(bf16[4,4,1,8,8192]{4,3,2,1,0:T(8,128)(2,1)} %param.18), kind=kLoop, calls=%fused_computation.96 | loop fusion | flops 3145712 | bytes 2097216 | tf_op jit(solution)/shard_map/reduce_sum | solution.py:51
  7.5 19.1 %all-reduce = (f32[]{:T(128)}, f32[]{:T(128)}, f32[]{:T(128)}, f32[]{:T(128)}, f32[]{:T(128)}, /*index=5*/f32[]{:T(128)}, f32[]{:T(128)}, f32[]{:T(128)}, f32[]{...) all-reduce(f32[]{:T(128)} %get-tuple-element.150, ...), channel_id=1, replica_groups=mesh['rep'=4,'shard'=8] {'shard'}, use_global_device_ids=true, to_apply=%region_7.0 | all-reduce | flops 16 | bytes 128 | tf_op jit(solution)/shard_map/psum | solution.py:51
  38.0 2.0 %fusion.108 = (bf16[1,8,8192]{2,1,0:T(8,128)(2,1)S(1)}, bf16[1,8,8192]{2,1,0:T(8,128)(2,1)S(1)}) fusion(f32[1,8,8192]{2,1,0:T(8,128)} %param.14, bf16[4,4,1,8,8192]{4,3,2,1,0:T(8,128)(2,1)S(1)} %copy-done, f32[]{:T(128)S(6)} %div.102, f32[]{:T(128)S(6)} %div.100, f32[]{:T(128)S(6)} %div.98, f32[1,8,8192]{2,1,0:T(8,128)} %param.17, f32[]{:T(128)S(6)} %div.96, ...), kind=kLoop, calls=%fused_computation.163 | loop fusion | flops 4128768 | bytes 1572880 | tf_op jit(solution)/shard_map/convert_element_type | solution.py:60
  40.0 6.7 %conditional.16 = (bf16[1,8,8192]{2,1,0:T(8,128)(2,1)}, bf16[1,8,8192]{2,1,0:T(8,128)(2,1)}) conditional(s32[]{:T(128)} %bitcast, (bf16[1,8,8192]{2,1,0:T(8,128)(2,1)S(1)}, bf16[1,8,8192]{2,1,0:T(8,128)(2,1)S(1)}) %tuple.96, (bf16[1,8,8192]{2,1,0:T(8,128)(2,1)S(1)}, bf16[1,8,8192]{2,1,0:T(8,128)(2,1)S(1)}) %tuple.96), branch_computations={%region_8.0_spmd, %region_9.0_spmd} | conditional | bytes 1048672
  40.0 1.6 %collective-permute-start.2 = (bf16[1,8,8192]{2,1,0:T(8,128)(2,1)S(1)}, bf16[1,8,8192]{2,1,0:T(8,128)(2,1)}, u32[]{:S(2)}, u32[]{:S(2)}) collective-permute-start(bf16[1,8,8192]{2,1,0:T(8,128)(2,1)S(1)} %get-tuple-element.82), channel_id=1, source_target_pairs={{0,16},{8,24},{16,0},{24,8},{1,17},{9,25},{17,1},{25,9},{2,18},{10... | collective-permute-start | bytes 393224 | tf_op jit(solution)/shard_map/cond/branch_1_fun/ppermute | solution.py:30
  42.1 3.0 %collective-permute-done.2 = bf16[1,8,8192]{2,1,0:T(8,128)(2,1)} collective-permute-done((bf16[1,8,8192]{2,1,0:T(8,128)(2,1)S(1)}, bf16[1,8,8192]{2,1,0:T(8,128)(2,1)}, u32[]{:S(2)}, u32[]{:S(2)}) %collective-permute-start.2) | collective-permute-done | bytes 131104 | tf_op jit(solution)/shard_map/cond/branch_1_fun/ppermute | solution.py:30
  45.2 1.5 %collective-permute-done.3 = bf16[1,8,8192]{2,1,0:T(8,128)(2,1)} collective-permute-done((bf16[1,8,8192]{2,1,0:T(8,128)(2,1)S(1)}, bf16[1,8,8192]{2,1,0:T(8,128)(2,1)}, u32[]{:S(2)}, u32[]{:S(2)}) %collective-permute-start.3) | collective-permute-done | bytes 131104 | tf_op jit(solution)/shard_map/cond/branch_1_fun/ppermute | solution.py:30
  47.8 1.8 %subtract_convert_fusion.2 = bf16[1,8,8192]{2,1,0:T(8,128)(2,1)} fusion(f32[1,8,8192]{2,1,0:T(8,128)S(1)} %get-tuple-element.185, f32[]{:T(128)S(6)} %div.110, f32[]{:T(128)S(6)} %div.108, f32[]{:T(128)S(6)} %div.106, f32[]{:T(128)S(6)} %div.104, f32[]{:T(128)S(6)} %div.102, f32[]{:T(128)S(6)} %div.100, f32[]{:T(128)S(6)} %div.98, ...), kind=kLoop, calls=%fused_computation.156 | loop fusion | flops 6422528 | bytes 1966112 | tf_op jit(solution)/shard_map/convert_element_type | solution.py:59
  49.6 6.7 %conditional.17 = (bf16[1,8,8192]{2,1,0:T(8,128)(2,1)}, bf16[1,8,8192]{2,1,0:T(8,128)(2,1)}) conditional(s32[]{:T(128)} %bitcast.5, (bf16[1,8,8192]{2,1,0:T(8,128)(2,1)}, bf16[1,8,8192]{2,1,0:T(8,128)(2,1)S(1)}) %tuple.97, (bf16[1,8,8192]{2,1,0:T(8,128)(2,1)}, bf16[1,8,8192]{2,1,0:T(8,128)(2,1)S(1)}) %tuple.97), branch_computations={%region_18.0_spmd, %region_19.0_spmd} | conditional | bytes 1048672
  49.6 1.5 %collective-permute-start.4 = (bf16[1,8,8192]{2,1,0:T(8,128)(2,1)}, bf16[1,8,8192]{2,1,0:T(8,128)(2,1)}, u32[]{:S(2)}, u32[]{:S(2)}) collective-permute-start(bf16[1,8,8192]{2,1,0:T(8,128)(2,1)} %get-tuple-element.84), channel_id=1, source_target_pairs={{0,8},{8,0},{16,24},{24,16},{1,9},{9,1},{17,25},{25,17},{2,10},{10... | collective-permute-start | bytes 393224 | tf_op jit(solution)/shard_map/cond/branch_0_fun/ppermute | solution.py:30
  51.6 3.3 %collective-permute-done.4 = bf16[1,8,8192]{2,1,0:T(8,128)(2,1)} collective-permute-done((bf16[1,8,8192]{2,1,0:T(8,128)(2,1)}, bf16[1,8,8192]{2,1,0:T(8,128)(2,1)}, u32[]{:S(2)}, u32[]{:S(2)}) %collective-permute-start.4) | collective-permute-done | bytes 131104 | tf_op jit(solution)/shard_map/cond/branch_0_fun/ppermute | solution.py:30
  54.9 1.4 %collective-permute-done.5 = bf16[1,8,8192]{2,1,0:T(8,128)(2,1)} collective-permute-done((bf16[1,8,8192]{2,1,0:T(8,128)(2,1)S(1)}, bf16[1,8,8192]{2,1,0:T(8,128)(2,1)}, u32[]{:S(2)}, u32[]{:S(2)}) %collective-permute-start.5) | collective-permute-done | bytes 131104 | tf_op jit(solution)/shard_map/cond/branch_0_fun/ppermute | solution.py:30
  57.5 2.2 %subtract_convert_fusion.1 = (bf16[1,8,8192]{2,1,0:T(8,128)(2,1)S(1)}, f32[1,8,8192]{2,1,0:T(8,128)}, f32[1,8,8192]{2,1,0:T(8,128)}) fusion(f32[1,8,8192]{2,1,0:T(8,128)S(1)} %get-tuple-element.180, f32[]{:T(128)S(6)} %div.118, f32[]{:T(128)S(6)} %div.116, f32[]{:T(128)S(6)} %div.114, bf16[4,4,1,8,8192]{4,3,2,1,0:T(8,128)(2,1)S(1)} %copy-done, ...), kind=kLoop, calls=%fused_computation.154 | loop fusion | flops 8781824 | bytes 3014704 | tf_op jit(solution)/shard_map/convert_element_type | solution.py:59
  59.7 6.5 %conditional.18 = (bf16[1,8,8192]{2,1,0:T(8,128)(2,1)}, bf16[1,8,8192]{2,1,0:T(8,128)(2,1)}) conditional(s32[]{:T(128)} %bitcast.10, (bf16[1,8,8192]{2,1,0:T(8,128)(2,1)S(1)}, bf16[1,8,8192]{2,1,0:T(8,128)(2,1)S(1)}) %tuple.98, (bf16[1,8,8192]{2,1,0:T(8,128)(2,1)S(1)}, bf16[1,8,8192]{2,1,0:T(8,128)(2,1)S(1)}) %tuple.98), branch_computations={%region_28.0_spmd, %region_29.0_spmd} | conditional | bytes 1048672
  59.7 1.4 %collective-permute-start.10 = (bf16[1,8,8192]{2,1,0:T(8,128)(2,1)S(1)}, bf16[1,8,8192]{2,1,0:T(8,128)(2,1)}, u32[]{:S(2)}, u32[]{:S(2)}) collective-permute-start(bf16[1,8,8192]{2,1,0:T(8,128)(2,1)S(1)} %get-tuple-element.90), channel_id=1, source_target_pairs={{0,16},{8,24},{16,0},{24,8},{1,17},{9,25},{17,1},{25,9},{2,18},{10... | collective-permute-start | bytes 393224 | tf_op jit(solution)/shard_map/cond/branch_1_fun/ppermute | solution.py:30
  61.7 3.0 %collective-permute-done.10 = bf16[1,8,8192]{2,1,0:T(8,128)(2,1)} collective-permute-done((bf16[1,8,8192]{2,1,0:T(8,128)(2,1)S(1)}, bf16[1,8,8192]{2,1,0:T(8,128)(2,1)}, u32[]{:S(2)}, u32[]{:S(2)}) %collective-permute-start.10) | collective-permute-done | bytes 131104 | tf_op jit(solution)/shard_map/cond/branch_1_fun/ppermute | solution.py:30
  64.8 1.4 %collective-permute-done.11 = bf16[1,8,8192]{2,1,0:T(8,128)(2,1)} collective-permute-done((bf16[1,8,8192]{2,1,0:T(8,128)(2,1)S(1)}, bf16[1,8,8192]{2,1,0:T(8,128)(2,1)}, u32[]{:S(2)}, u32[]{:S(2)}) %collective-permute-start.11) | collective-permute-done | bytes 131104 | tf_op jit(solution)/shard_map/cond/branch_1_fun/ppermute | solution.py:30
  67.6 2.8 %subtract_convert_fusion = (bf16[1,8,8192]{2,1,0:T(8,128)(2,1)S(1)}, f32[1,8,8192]{2,1,0:T(8,128)}, f32[1,8,8192]{2,1,0:T(8,128)}) fusion(f32[1,8,8192]{2,1,0:T(8,128)S(1)} %get-tuple-element.175, f32[1,8,8192]{2,1,0:T(8,128)} %get-tuple-element.183, f32[]{:T(128)S(6)} %div.124, f32[1,8,8192]{2,1,0:T(8,128)} %get-tuple-element.182, f32[]{:T(128)S(6)} %div.122, ...), kind=kLoop, calls=%fused_computation.152 | loop fusion | flops 5832704 | bytes 2359324 | tf_op jit(solution)/shard_map/convert_element_type | solution.py:59
  70.4 6.6 %conditional.19 = (bf16[1,8,8192]{2,1,0:T(8,128)(2,1)}, bf16[1,8,8192]{2,1,0:T(8,128)(2,1)}) conditional(s32[]{:T(128)} %bitcast.15, (bf16[1,8,8192]{2,1,0:T(8,128)(2,1)S(1)}, bf16[1,8,8192]{2,1,0:T(8,128)(2,1)S(1)}) %tuple.99, (bf16[1,8,8192]{2,1,0:T(8,128)(2,1)S(1)}, bf16[1,8,8192]{2,1,0:T(8,128)(2,1)S(1)}) %tuple.99), branch_computations={%region_38.0_spmd, %region_39.0_spmd} | conditional | bytes 1048672
  70.4 1.5 %collective-permute-start.12 = (bf16[1,8,8192]{2,1,0:T(8,128)(2,1)S(1)}, bf16[1,8,8192]{2,1,0:T(8,128)(2,1)}, u32[]{:S(2)}, u32[]{:S(2)}) collective-permute-start(bf16[1,8,8192]{2,1,0:T(8,128)(2,1)S(1)} %get-tuple-element.92), channel_id=1, source_target_pairs={{0,8},{8,0},{16,24},{24,16},{1,9},{9,1},{17,25},{25,17},{2,10},{10... | collective-permute-start | bytes 393224 | tf_op jit(solution)/shard_map/cond/branch_0_fun/ppermute | solution.py:30
  72.4 3.0 %collective-permute-done.12 = bf16[1,8,8192]{2,1,0:T(8,128)(2,1)} collective-permute-done((bf16[1,8,8192]{2,1,0:T(8,128)(2,1)S(1)}, bf16[1,8,8192]{2,1,0:T(8,128)(2,1)}, u32[]{:S(2)}, u32[]{:S(2)}) %collective-permute-start.12) | collective-permute-done | bytes 131104 | tf_op jit(solution)/shard_map/cond/branch_0_fun/ppermute | solution.py:30
  75.5 1.5 %collective-permute-done.13 = bf16[1,8,8192]{2,1,0:T(8,128)(2,1)} collective-permute-done((bf16[1,8,8192]{2,1,0:T(8,128)(2,1)S(1)}, bf16[1,8,8192]{2,1,0:T(8,128)(2,1)}, u32[]{:S(2)}, u32[]{:S(2)}) %collective-permute-start.13) | collective-permute-done | bytes 131104 | tf_op jit(solution)/shard_map/cond/branch_0_fun/ppermute | solution.py:30
  77.0 2.3 %fusion.83 = (f32[1,8,8192]{2,1,0:T(8,128)}, f32[1,8,8192]{2,1,0:T(8,128)}) fusion(f32[1,8,8192]{2,1,0:T(8,128)S(1)} %get-tuple-element.175, bf16[1,8,8192]{2,1,0:T(8,128)(2,1)} %get-tuple-element.138, bf16[1,8,8192]{2,1,0:T(8,128)(2,1)} %get-tuple-element.139, bf16[1,8,8192]{2,1,0:T(8,128)(2,1)S(1)} %get-tuple-element.176, ...), kind=kLoop, calls=%fused_computation.133 | loop fusion | flops 2097152 | bytes 2228224 | tf_op jit(solution)/shard_map/sub | solution.py:74
  (17 shorter events, 6.0 us)
Async XLA Ops:
  0.6 37.4 %copy-start = (bf16[4,4,1,8,8192]{4,3,2,1,0:T(8,128)(2,1)S(1)}, bf16[4,4,1,8,8192]{4,3,2,1,0:T(8,128)(2,1)}, u32[]{:S(2)}) copy-start(bf16[4,4,1,8,8192]{4,3,2,1,0:T(8,128)(2,1)} %param.18) | copy-start | bytes 6291460
  0.6 46.1 %copy-start.1 = (f32[1,8,8192]{2,1,0:T(8,128)S(1)}, f32[1,8,8192]{2,1,0:T(8,128)}, u32[]{:S(2)}) copy-start(f32[1,8,8192]{2,1,0:T(8,128)} %param.15) | copy-start | bytes 786436
  0.7 46.0 %copy-start.4 = (f32[1,8,8192]{2,1,0:T(8,128)S(1)}, f32[1,8,8192]{2,1,0:T(8,128)}, u32[]{:S(2)}) copy-start(f32[1,8,8192]{2,1,0:T(8,128)} %param.14) | copy-start | bytes 786436
  4.7 43.1 %copy-start.2 = (f32[1,8,8192]{2,1,0:T(8,128)S(1)}, f32[1,8,8192]{2,1,0:T(8,128)}, u32[]{:S(2)}) copy-start(f32[1,8,8192]{2,1,0:T(8,128)} %param.17) | copy-start | bytes 786436
  4.7 43.1 %copy-start.3 = (f32[1,8,8192]{2,1,0:T(8,128)S(1)}, f32[1,8,8192]{2,1,0:T(8,128)}, u32[]{:S(2)}) copy-start(f32[1,8,8192]{2,1,0:T(8,128)} %param.16) | copy-start | bytes 786436
  40.0 5.1 %collective-permute-start.2 = (bf16[1,8,8192]{2,1,0:T(8,128)(2,1)S(1)}, bf16[1,8,8192]{2,1,0:T(8,128)(2,1)}, u32[]{:S(2)}, u32[]{:S(2)}) collective-permute-start(bf16[1,8,8192]{2,1,0:T(8,128)(2,1)S(1)} %get-tuple-element.82), channel_id=1, source_target_pairs={{0,16},{8,24},{16,0},{24,8},{1,17},{9,25},{17,1},{25,9},{2,18},{10... | collective-permute-start | bytes 393224 | tf_op jit(solution)/shard_map/cond/branch_1_fun/ppermute | solution.py:30
  41.6 5.1 %collective-permute-start.3 = (bf16[1,8,8192]{2,1,0:T(8,128)(2,1)S(1)}, bf16[1,8,8192]{2,1,0:T(8,128)(2,1)}, u32[]{:S(2)}, u32[]{:S(2)}) collective-permute-start(bf16[1,8,8192]{2,1,0:T(8,128)(2,1)S(1)} %get-tuple-element.83), channel_id=1, source_target_pairs={{0,16},{8,24},{16,0},{24,8},{1,17},{9,25},{17,1},{25,9},{2,18},{10... | collective-permute-start | bytes 393224 | tf_op jit(solution)/shard_map/cond/branch_1_fun/ppermute | solution.py:30
  49.6 5.3 %collective-permute-start.4 = (bf16[1,8,8192]{2,1,0:T(8,128)(2,1)}, bf16[1,8,8192]{2,1,0:T(8,128)(2,1)}, u32[]{:S(2)}, u32[]{:S(2)}) collective-permute-start(bf16[1,8,8192]{2,1,0:T(8,128)(2,1)} %get-tuple-element.84), channel_id=1, source_target_pairs={{0,8},{8,0},{16,24},{24,16},{1,9},{9,1},{17,25},{25,17},{2,10},{10... | collective-permute-start | bytes 393224 | tf_op jit(solution)/shard_map/cond/branch_0_fun/ppermute | solution.py:30
  51.1 5.2 %collective-permute-start.5 = (bf16[1,8,8192]{2,1,0:T(8,128)(2,1)S(1)}, bf16[1,8,8192]{2,1,0:T(8,128)(2,1)}, u32[]{:S(2)}, u32[]{:S(2)}) collective-permute-start(bf16[1,8,8192]{2,1,0:T(8,128)(2,1)S(1)} %get-tuple-element.85), channel_id=1, source_target_pairs={{0,8},{8,0},{16,24},{24,16},{1,9},{9,1},{17,25},{25,17},{2,10},{10... | collective-permute-start | bytes 393224 | tf_op jit(solution)/shard_map/cond/branch_0_fun/ppermute | solution.py:30
  59.7 5.1 %collective-permute-start.10 = (bf16[1,8,8192]{2,1,0:T(8,128)(2,1)S(1)}, bf16[1,8,8192]{2,1,0:T(8,128)(2,1)}, u32[]{:S(2)}, u32[]{:S(2)}) collective-permute-start(bf16[1,8,8192]{2,1,0:T(8,128)(2,1)S(1)} %get-tuple-element.90), channel_id=1, source_target_pairs={{0,16},{8,24},{16,0},{24,8},{1,17},{9,25},{17,1},{25,9},{2,18},{10... | collective-permute-start | bytes 393224 | tf_op jit(solution)/shard_map/cond/branch_1_fun/ppermute | solution.py:30
  61.1 5.1 %collective-permute-start.11 = (bf16[1,8,8192]{2,1,0:T(8,128)(2,1)S(1)}, bf16[1,8,8192]{2,1,0:T(8,128)(2,1)}, u32[]{:S(2)}, u32[]{:S(2)}) collective-permute-start(bf16[1,8,8192]{2,1,0:T(8,128)(2,1)S(1)} %get-tuple-element.91), channel_id=1, source_target_pairs={{0,16},{8,24},{16,0},{24,8},{1,17},{9,25},{17,1},{25,9},{2,18},{10... | collective-permute-start | bytes 393224 | tf_op jit(solution)/shard_map/cond/branch_1_fun/ppermute | solution.py:30
  70.4 5.1 %collective-permute-start.12 = (bf16[1,8,8192]{2,1,0:T(8,128)(2,1)S(1)}, bf16[1,8,8192]{2,1,0:T(8,128)(2,1)}, u32[]{:S(2)}, u32[]{:S(2)}) collective-permute-start(bf16[1,8,8192]{2,1,0:T(8,128)(2,1)S(1)} %get-tuple-element.92), channel_id=1, source_target_pairs={{0,8},{8,0},{16,24},{24,16},{1,9},{9,1},{17,25},{25,17},{2,10},{10... | collective-permute-start | bytes 393224 | tf_op jit(solution)/shard_map/cond/branch_0_fun/ppermute | solution.py:30
  71.9 5.1 %collective-permute-start.13 = (bf16[1,8,8192]{2,1,0:T(8,128)(2,1)S(1)}, bf16[1,8,8192]{2,1,0:T(8,128)(2,1)}, u32[]{:S(2)}, u32[]{:S(2)}) collective-permute-start(bf16[1,8,8192]{2,1,0:T(8,128)(2,1)S(1)} %get-tuple-element.93), channel_id=1, source_target_pairs={{0,8},{8,0},{16,24},{24,16},{1,9},{9,1},{17,25},{25,17},{2,10},{10... | collective-permute-start | bytes 393224 | tf_op jit(solution)/shard_map/cond/branch_0_fun/ppermute | solution.py:30
where the time goes:
time: 79.7 us; the launch traced here: 79.3 us
  blocking collectives  19.1 us (24%)
  waiting for transfers between devices  18.2 us (23%)
  other arithmetic  17.6 us (22%)
  between operations  14.7 us (18%)
  starting transfers between devices  8.17 us (10%)
  local copies, waits for them, and re-layouts  1.48 us (2%)
    psum x1, blocking collectives, on_device(): square_sum = lax.psum(jnp.sum(gradient * gradient), 'shard')  19.1 us
    ppermute x8, waiting for transfers between devices, swapped(): return lax.ppermute(value, axis, pairs)  18.2 us
    ppermute x8, starting transfers between devices, swapped(): return lax.ppermute(value, axis, pairs)  8.17 us
    convert_element_type x3, other arithmetic, on_device(): pseudo_grad = (slow_now - fast_weights).astype(jnp.bfloat16)  6.76 us
    convert_element_type x4, other arithmetic, on_device(): sent_slow = slow_now.astype(jnp.bfloat16)  5.78 us
    reduce_sum x1, other arithmetic, on_device(): square_sum = lax.psum(jnp.sum(gradient * gradient), 'shard')  2.77 us
    sub x1, other arithmetic, on_device(): slow_now + mix_rate * (other_slow - slow_now)  2.27 us
  transfers between devices with their start and end apart: 8, of which 8 were waited for; matrix products, arithmetic and copies ran while one was open for 0% of the time, Pallas kernels for 0%

commit v1 on v0

--- a/solution.py
+++ b/solution.py
@@ -3,6 +3,8 @@
 import jax
 import jax.numpy as jnp
 from jax import lax
+from jax.experimental import pallas as pl
+from jax.experimental.pallas import tpu as pltpu
 from jax.sharding import PartitionSpec as P
 
 clip_limit = 1.0
@@ -14,6 +16,12 @@
 outer_rate = 0.7
 momentum_rate = 0.9
 mix_rate = 0.25
+tiny = 1e-30
+
+LANES = 128
+CHUNKS = 4
+GROUP = 4
+MESH = pl.DeviceIdType.MESH
 
 
 def shortened(value):
@@ -38,17 +46,19 @@
     )
 
 
-def on_device(slow_weights, outer_momentum, adam_first, adam_second, gradients, pair_mask):
+def step_by_step(slow_weights, outer_momentum, adam_first, adam_second, gradients, pair_mask):
     bit_count = lax.axis_size("rep").bit_length() - 1
     slow_now = slow_weights
     momentum = outer_momentum
     moment_one = adam_first
     moment_two = adam_second
+    wide = gradients.astype(jnp.float32)
+    square_sums = lax.psum(jnp.sum(wide * wide, axis=(2, 3, 4)), "shard")
     for outer_step in range(gradients.shape[0]):
         fast_weights = slow_now
         for inner_step in range(gradients.shape[1]):
             gradient = gradients[outer_step, inner_step].astype(jnp.float32)
-            square_sum = lax.psum(jnp.sum(gradient * gradient), "shard")
+            square_sum = square_sums[outer_step, inner_step]
             factor = clip_limit / jnp.maximum(jnp.sqrt(square_sum), clip_limit)
             clipped = factor * gradient
             moment_one = beta_one * moment_one + (1.0 - beta_one) * clipped
@@ -78,6 +88,349 @@
     return (slow_now, momentum, moment_one, moment_two)
 
 
+def scaled(factor, value):
+    return None if value is None else factor * value
+
+
+def added(left, right):
+    if left is None:
+        return right
+    return left if right is None else left + right
+
+
+def mixing(step_bits, outer, inner):
+    keep = 1.0 - inner_rate * decay_rate
+    pull = 1.0 - keep**inner
+    one = jnp.ones((8, LANES), jnp.float32)
+    spectrum = []
+    for char in range(4):
+        slow = [one] + [None] * (outer + 1)
+        moment = [None, one] + [None] * outer
+        for t in range(outer):
+            high = step_bits[t]
+            differs = (char & 1) * (1.0 - high) + (char >> 1) * high
+            same = 1.0 - differs
+            half = 1.0 - 2.0 * mix_rate * differs
+            average = [scaled(pull * same, part) for part in slow]
+            average[2 + t] = same * one
+            moment = [
+                added(scaled(momentum_rate, part), mean) for part, mean in zip(moment, average)
+            ]
+            slow = [
+                added(
+                    scaled(half, part),
+                    added(scaled(-outer_rate, mean), scaled(-outer_rate * momentum_rate, push)),
+                )
+                for part, mean, push in zip(slow, average, moment)
+            ]
+        spectrum.append((slow, moment))
+    table = []
+    for d in range(4):
+        rows = []
+        for output in range(2):
+            row = []
+            for source in range(outer + 2):
+                value = None
+                for char in range(4):
+                    sign = -0.25 if bin(char & d).count("1") % 2 else 0.25
+                    value = added(value, scaled(sign, spectrum[char][output][source]))
+                row.append(value)
+            rows.append(row)
+        table.append(rows)
+    return table
+
+
+def kernel(
+    shards,
+    mask_ref,
+    slow_ref,
+    momentum_ref,
+    first_ref,
+    second_ref,
+    grad_ref,
+    new_slow_ref,
+    new_momentum_ref,
+    new_first_ref,
+    new_second_ref,
+    coef,
+    clips,
+    sums,
+    relay_out,
+    relay_in,
+    last_out,
+    last_in,
+    near_out,
+    near_in,
+    sum_send,
+    sum_recv,
+    relay_send,
+    relay_recv,
+    last_send,
+    last_recv,
+    near_send,
+    near_recv,
+):
+    outer, inner = grad_ref.shape[0], grad_ref.shape[1]
+    columns = slow_ref.shape[-1]
+    steps = outer * inner
+    width = last_out.shape[-1]
+    pieces = columns // width
+    rep = lax.axis_index("rep")
+    shard = lax.axis_index("shard")
+    low_partner = rep + 1 - 2 * (rep % 2)
+    high_partner = rep + 2 - 4 * ((rep // 2) % 2)
+
+    barrier = pltpu.get_barrier_semaphore()
+    for partner in (low_partner, high_partner):
+        pl.semaphore_signal(barrier, inc=1, device_id=(partner, shard), device_id_type=MESH)
+    for offset in range(1, shards):
+        peer = lax.rem(shard + offset, shards)
+        pl.semaphore_signal(barrier, inc=1, device_id=(rep, peer), device_id_type=MESH)
+
+    span = LANES * GROUP
+
+    def squares(i, totals):
+        totals = list(totals)
+        for part in range(GROUP):
+            at = pl.ds(pl.multiple_of(i * span + part * LANES, LANES), LANES)
+            for j in range(steps):
+                grad = grad_ref[j // inner, j % inner, 0, :, at].astype(jnp.float32)
+                totals[j] = totals[j] + grad * grad
+        return tuple(totals)
+
+    zero = jnp.zeros((8, LANES), jnp.float32)
+    totals = lax.fori_loop(0, columns // span, squares, (zero,) * steps)
+    lane = lax.broadcasted_iota(jnp.int32, (1, LANES), 1)
+    share = jnp.zeros((1, LANES), jnp.float32)
+    for j in range(steps):
+        column = jnp.sum(totals[j], axis=0, keepdims=True)
+        share = jnp.where(lane == j, jnp.sum(column, axis=1, keepdims=True), share)
+    sums[0] = share
+
+    pl.semaphore_wait(barrier, shards + 1)
+    copies = []
+    for offset in range(1, shards):
+        peer = lax.rem(shard + offset, shards)
+        copies.append(
+            pltpu.make_async_remote_copy(
+                src_ref=sums.at[0],
+                dst_ref=sums.at[offset],
+                send_sem=sum_send.at[offset],
+                recv_sem=sum_recv.at[offset],
+                device_id=(rep, peer),
+                device_id_type=MESH,
+            )
+        )
+        copies[-1].start()
+
+    bits = [
+        jnp.full((8, LANES), mask_ref[t] - 1, jnp.int32).astype(jnp.float32) for t in range(outer)
+    ]
+    table = mixing(bits, outer, inner)
+    sources = outer + 2
+    for d in range(4):
+        for output in range(2):
+            for source in range(sources):
+                coef[(d * 2 + output) * sources + source] = table[d][output][source]
+
+    for copy in copies:
+        copy.wait_recv()
+    square_sum = sums[0]
+    for offset in range(1, shards):
+        square_sum = square_sum + sums[offset]
+    factor = clip_limit / jnp.maximum(jnp.sqrt(square_sum), clip_limit)
+    for j in range(steps):
+        clips[j] = jnp.broadcast_to(factor[:, j : j + 1], (8, LANES))
+
+    keep = 1.0 - inner_rate * decay_rate
+
+    def relay(j):
+        return pltpu.make_async_remote_copy(
+            src_ref=relay_out.at[j],
+            dst_ref=relay_in.at[j],
+            send_sem=relay_send.at[j],
+            recv_sem=relay_recv.at[j],
+            device_id=(low_partner + (j % 2) * (high_partner - low_partner), shard),
+            device_id_type=MESH,
+        )
+
+    def near(j):
+        return pltpu.make_async_remote_copy(
+            src_ref=near_out.at[j],
+            dst_ref=near_in.at[j],
+            send_sem=near_send.at[j],
+            recv_sem=near_recv.at[j],
+            device_id=(low_partner + (j % 2) * (high_partner - low_partner), shard),
+            device_id_type=MESH,
+        )
+
+    def last(j):
+        return pltpu.make_async_remote_copy(
+            src_ref=last_out.at[j],
+            dst_ref=last_in.at[j],
+            send_sem=last_send.at[j],
+            recv_sem=last_recv.at[j],
+            device_id=(high_partner - (j % 2) * (high_partner - low_partner), shard),
+            device_id_type=MESH,
+        )
+
+    def updates(j, group):
+        base = j * width + group * span
+        inside = group * span
+        firsts, seconds, moves = [], [], []
+        spots = [pl.ds(pl.multiple_of(base + p * LANES, LANES), LANES) for p in range(GROUP)]
+        for at in spots:
+            firsts.append(first_ref[0, :, at])
+            seconds.append(second_ref[0, :, at])
+            moves.append([])
+        for t in range(outer):
+            move = [None] * GROUP
+            for k in range(inner):
+                clip = clips[t * inner + k]
+                gain_one = (1.0 - beta_one) * clip
+                gain_two = (1.0 - beta_two) * clip * clip
+                for p, at in enumerate(spots):
+                    grad = grad_ref[t, k, 0, :, at].astype(jnp.float32)
+                    firsts[p] = beta_one * firsts[p] + gain_one * grad
+                    seconds[p] = beta_two * seconds[p] + gain_two * (grad * grad)
+                    floor = jnp.maximum(seconds[p], tiny)
+                    bottom = floor * lax.rsqrt(floor) + adam_eps
+                    unit = firsts[p] / bottom
+                    move[p] = unit if move[p] is None else keep * move[p] + unit
+            for p in range(GROUP):
+                moves[p].append(inner_rate * move[p])
+        values = []
+        for p, at in enumerate(spots):
+            new_first_ref[0, :, at] = firsts[p]
+            new_second_ref[0, :, at] = seconds[p]
+            values.append([slow_ref[0, :, at], momentum_ref[0, :, at]] + moves[p])
+
+        def mixed(d):
+            out = []
+            for p in range(GROUP):
+                pair = []
+                for output in range(2):
+                    total = None
+                    for source in range(sources):
+                        weight = coef[(d * 2 + output) * sources + source]
+                        total = added(total, weight * values[p][source])
+                    pair.append(total)
+                out.append(pair)
+            return out
+
+        def stored(target, out):
+            for p in range(GROUP):
+                inside_at = pl.ds(pl.multiple_of(inside + p * LANES, LANES), LANES)
+                target[j, :, inside_at] = jnp.concatenate(out[p], axis=0).astype(jnp.bfloat16)
+
+        kind = j % 2
+        stored(relay_out, mixed(3))
+        stored(near_out, mixed(1 + kind))
+        stored(last_out, mixed(2 - kind))
+        for (slow, momentum), at in zip(mixed(0), spots):
+            new_slow_ref[0, :, at] = slow
+            new_momentum_ref[0, :, at] = momentum
+
+    def first_stage(j, carry):
+
+        def body(group, inside):
+            updates(j, group)
+            return inside
+
+        lax.fori_loop(0, width // span, body, 0)
+        relay(j).start()
+        near(j).start()
+        return carry
+
+    def second_stage(j, carry):
+        relay(j).wait_recv()
+        last_out[j] = (
+            last_out[j].astype(jnp.float32) + relay_in[j].astype(jnp.float32)
+        ).astype(jnp.bfloat16)
+        last(j).start()
+        return carry
+
+    def finish(j, carry):
+        near(j).wait_recv()
+        last(j).wait_recv()
+        at = pl.ds(pl.multiple_of(j * width, LANES), width)
+        arrived = near_in[j].astype(jnp.float32) + last_in[j].astype(jnp.float32)
+        new_slow_ref[0, :, at] += arrived[:8]
+        new_momentum_ref[0, :, at] += arrived[8:]
+        return carry
+
+    def both(j, carry):
+        first_stage(j, carry)
+        return second_stage(j - 2, carry)
+
+    lax.fori_loop(0, 2, first_stage, 0)
+    lax.fori_loop(2, pieces, both, 0)
+    lax.fori_loop(pieces - 2, pieces, second_stage, 0)
+    lax.fori_loop(0, pieces, finish, 0)
+
+    for copy in copies:
+        copy.wait_send()
+
+    def drained(j, carry):
+        relay(j).wait_send()
+        near(j).wait_send()
+        last(j).wait_send()
+        return carry
+
+    lax.fori_loop(0, pieces, drained, 0)
+
+
+def four_replicas(slow_weights, outer_momentum, adam_first, adam_second, gradients, pair_mask):
+    shards = lax.axis_size("shard")
+    outer, inner = gradients.shape[:2]
+    columns = slow_weights.shape[-1]
+    pieces = 2 * CHUNKS
+    width = columns // pieces
+    rows = 2 * slow_weights.shape[1]
+    piece = pltpu.VMEM((pieces, rows, width), jnp.bfloat16)
+    vmem = pl.BlockSpec(memory_space=pltpu.VMEM)
+    dma = pltpu.SemaphoreType.DMA
+    return pl.pallas_call(
+        partial(kernel, shards),
+        out_shape=[jax.ShapeDtypeStruct(slow_weights.shape, jnp.float32)] * 4,
+        in_specs=[pl.BlockSpec(memory_space=pltpu.SMEM)] + [vmem] * 5,
+        out_specs=[vmem] * 4,
+        scratch_shapes=[
+            pltpu.VMEM((8 * (outer + 2), 8, LANES), jnp.float32),
+            pltpu.VMEM((outer * inner, 8, LANES), jnp.float32),
+            pltpu.VMEM((shards, 1, LANES), jnp.float32),
+            piece,
+            piece,
+            piece,
+            piece,
+            piece,
+            piece,
+            dma((shards,)),
+            dma((shards,)),
+            dma((pieces,)),
+            dma((pieces,)),
+            dma((pieces,)),
+            dma((pieces,)),
+            dma((pieces,)),
+            dma((pieces,)),
+        ],
+        compiler_params=pltpu.CompilerParams(
+            collective_id=0, has_side_effects=True, vmem_limit_bytes=32 * 2**20
+        ),
+    )(pair_mask, slow_weights, outer_momentum, adam_first, adam_second, gradients)
+
+
+def on_device(*arguments):
+    slow_weights, gradients = arguments[0], arguments[4]
+    fits = (
+        lax.axis_size("rep") == 4
+        and slow_weights.shape[:2] == (1, 8)
+        and slow_weights.shape[2] % (2 * CHUNKS * GROUP * LANES) == 0
+        and gradients.shape[0] * gradients.shape[1] <= LANES
+    )
+    return four_replicas(*arguments) if fits else step_by_step(*arguments)
+
+
 def solution(mesh):
     return jax.shard_map(
         on_device,

time: 79.7 us -> 33.8 us (0.42)
  Pallas kernels: 0 us -> 24 us
  blocking collectives: 19.1 us -> 0 us
  waiting for transfers between devices: 18.2 us -> 0 us
  other arithmetic: 17.6 us -> 0 us
  between operations: 14.7 us -> 0.66 us
  starting transfers between devices: 8.17 us -> 0 us
  local copies, waits for them, and re-layouts: 1.48 us -> 8.85 us
    pallas_call x0 -> x1, Pallas kernels: none -> 24 us  [four_replicas(): pl.pallas_call(partial(kernel, shards), out_shape=[jax.ShapeDtypeStruct(s...]
    psum x1 -> x0, blocking collectives: 19.1 us -> none  [on_device(): square_sum = lax.psum(jnp.sum(gradient * gradient), 'shard')]
    ppermute x8 -> x0, waiting for transfers between devices: 18.2 us -> none  [swapped(): return lax.ppermute(value, axis, pairs)]
    convert_element_type x7 -> x0, other arithmetic: 12.5 us -> none  [the longest x3 6.76 us: on_device(): pseudo_grad = (slow_now - fast_weights).astype(jnp.bfloat16)]
    unnamed x10 -> x16, local copies, waits for them, and re-layouts: 0.03 us -> 8.85 us
    ppermute x8 -> x0, starting transfers between devices: 8.17 us -> none  [swapped(): return lax.ppermute(value, axis, pairs)]
    reduce_sum x1 -> x0, other arithmetic: 2.77 us -> none  [on_device(): square_sum = lax.psum(jnp.sum(gradient * gradient), 'shard')]
    sub x1 -> x0, other arithmetic: 2.27 us -> none  [on_device(): slow_now + mix_rate * (other_slow - slow_now)]
  transfers between devices with their start and end apart: 8 -> 0, of which waited for: 8 -> 0; matrix products, arithmetic and copies ran while one was open for 0% -> 0% of each run, Pallas kernels for 0% -> 0%
where the time goes in v1:
time: 33.8 us; the launch traced here: 33.5 us
  Pallas kernels  24 us (71%)
  local copies, waits for them, and re-layouts  8.85 us (26%)
  between operations  0.66 us (2%)
    pallas_call x1, Pallas kernels, four_replicas(): pl.pallas_call(partial(kernel, shards), out_shape=[jax.ShapeDtypeStruct(s...  24 us
    unnamed x16, local copies, waits for them, and re-layouts  8.85 us

profile of v1, /device:TPU:0, one launch (start us, length us, event | category | flops | bytes accessed | tf_op | source)
XLA Modules:
  0.0 33.5 jit_solution(12039062122156083431)
XLA Ops:
  0.6 0.0 copy-start
  0.6 1.6 %copy-done = bf16[4,4,1,8,8192]{4,3,2,1,0:T(8,128)(2,1)S(1)} copy-done((bf16[4,4,1,8,8192]{4,3,2,1,0:T(8,128)(2,1)S(1)}, bf16[4,4,1,8,8192]{4,3,2,1,0:T(8,128)(2,1)}, u32[]{:S(2)}) %copy-start) | copy-done | bytes 2097176
  2.2 0.0 copy-start.1
  2.2 0.9 %copy-done.1 = f32[1,8,8192]{2,1,0:T(8,128)S(1)} copy-done((f32[1,8,8192]{2,1,0:T(8,128)S(1)}, f32[1,8,8192]{2,1,0:T(8,128)}, u32[]{:S(2)}) %copy-start.1) | copy-done | bytes 262168
  3.2 0.0 copy-start.2
  3.2 0.9 %copy-done.2 = f32[1,8,8192]{2,1,0:T(8,128)S(1)} copy-done((f32[1,8,8192]{2,1,0:T(8,128)S(1)}, f32[1,8,8192]{2,1,0:T(8,128)}, u32[]{:S(2)}) %copy-start.2) | copy-done | bytes 262168
  4.1 0.0 copy-start.3
  4.1 0.9 %copy-done.3 = f32[1,8,8192]{2,1,0:T(8,128)S(1)} copy-done((f32[1,8,8192]{2,1,0:T(8,128)S(1)}, f32[1,8,8192]{2,1,0:T(8,128)}, u32[]{:S(2)}) %copy-start.3) | copy-done | bytes 262168
  5.1 0.0 copy-start.4
  5.1 0.9 %copy-done.4 = f32[1,8,8192]{2,1,0:T(8,128)S(1)} copy-done((f32[1,8,8192]{2,1,0:T(8,128)S(1)}, f32[1,8,8192]{2,1,0:T(8,128)}, u32[]{:S(2)}) %copy-start.4) | copy-done | bytes 262168
  6.0 0.0 copy-start.5
  6.0 0.7 %copy-done.5 = s32[4]{0:T(128)S(1)} copy-done((s32[4]{0:T(128)S(1)}, s32[4]{0:T(128)}, u32[]{:S(2)}) %copy-start.5) | copy-done | bytes 40
  6.7 24.0 %shard_map.93 = (f32[1,8,8192]{2,1,0:T(8,128)S(1)}, f32[1,8,8192]{2,1,0:T(8,128)S(1)}, f32[1,8,8192]{2,1,0:T(8,128)S(1)}, f32[1,8,8192]{2,1,0:T(8,128)S(1)}) custom-call(s32[4]{0:T(128)S(1)} %copy-done.5, f32[1,8,8192]{2,1,0:T(8,128)S(1)} %copy-done.1, f32[1,8,8192]{2,1,0:T(8,128)S(1)} %copy-done.2, f32[1,8,8192]{2,1,0:T(8,128)S(1)} %copy-done.3, ...), custom_call_target="tpu_custom_call" | custom-call | tf_op jit(solution)/shard_map/pallas_call | solution.py:393
  30.7 0.7 %copy.14 = f32[1,8,8192]{2,1,0:T(8,128)} copy(f32[1,8,8192]{2,1,0:T(8,128)S(1)} %get-tuple-element.8) | data formatting | bytes 524288
  31.4 0.7 %copy.15 = f32[1,8,8192]{2,1,0:T(8,128)} copy(f32[1,8,8192]{2,1,0:T(8,128)S(1)} %get-tuple-element.9) | data formatting | bytes 524288
  32.1 0.7 %copy.16 = f32[1,8,8192]{2,1,0:T(8,128)} copy(f32[1,8,8192]{2,1,0:T(8,128)S(1)} %get-tuple-element.10) | data formatting | bytes 524288
  32.8 0.7 %copy.17 = f32[1,8,8192]{2,1,0:T(8,128)} copy(f32[1,8,8192]{2,1,0:T(8,128)S(1)} %get-tuple-element.11) | data formatting | bytes 524288
Async XLA Ops:
  0.6 1.6 %copy-start = (bf16[4,4,1,8,8192]{4,3,2,1,0:T(8,128)(2,1)S(1)}, bf16[4,4,1,8,8192]{4,3,2,1,0:T(8,128)(2,1)}, u32[]{:S(2)}) copy-start(bf16[4,4,1,8,8192]{4,3,2,1,0:T(8,128)(2,1)} %grad_ref.1) | copy-start | bytes 6291460
  2.2 0.9 %copy-start.1 = (f32[1,8,8192]{2,1,0:T(8,128)S(1)}, f32[1,8,8192]{2,1,0:T(8,128)}, u32[]{:S(2)}) copy-start(f32[1,8,8192]{2,1,0:T(8,128)} %slow_ref.1) | copy-start | bytes 786436
  3.2 0.9 %copy-start.2 = (f32[1,8,8192]{2,1,0:T(8,128)S(1)}, f32[1,8,8192]{2,1,0:T(8,128)}, u32[]{:S(2)}) copy-start(f32[1,8,8192]{2,1,0:T(8,128)} %momentum_ref.1) | copy-start | bytes 786436
  4.1 0.9 %copy-start.3 = (f32[1,8,8192]{2,1,0:T(8,128)S(1)}, f32[1,8,8192]{2,1,0:T(8,128)}, u32[]{:S(2)}) copy-start(f32[1,8,8192]{2,1,0:T(8,128)} %first_ref.1) | copy-start | bytes 786436
  5.1 0.9 %copy-start.4 = (f32[1,8,8192]{2,1,0:T(8,128)S(1)}, f32[1,8,8192]{2,1,0:T(8,128)}, u32[]{:S(2)}) copy-start(f32[1,8,8192]{2,1,0:T(8,128)} %second_ref.1) | copy-start | bytes 786436
  6.0 0.7 %copy-start.5 = (s32[4]{0:T(128)S(1)}, s32[4]{0:T(128)}, u32[]{:S(2)}) copy-start(s32[4]{0:T(128)} %mask_ref.1) | copy-start | bytes 52

commit v2 on v1

--- a/solution.py
+++ b/solution.py
@@ -20,7 +20,8 @@
 
 LANES = 128
 CHUNKS = 4
-GROUP = 4
+GROUP = 8
+EARLY = 4
 MESH = pl.DeviceIdType.MESH
 
 
@@ -152,15 +153,20 @@
     new_momentum_ref,
     new_first_ref,
     new_second_ref,
+    near_in,
+    last_in,
     coef,
-    clips,
+    gains,
     sums,
+    grads,
+    states,
     relay_out,
     relay_in,
+    last_sum,
     last_out,
-    last_in,
     near_out,
-    near_in,
+    grad_load,
+    state_load,
     sum_send,
     sum_recv,
     relay_send,
@@ -180,6 +186,14 @@
     low_partner = rep + 1 - 2 * (rep % 2)
     high_partner = rep + 2 - 4 * ((rep // 2) % 2)
 
+    loads = [
+        pltpu.make_async_copy(grad_ref.at[t], grads.at[t], grad_load.at[t]) for t in range(outer)
+    ]
+    for i, ref in enumerate((slow_ref, momentum_ref, first_ref, second_ref)):
+        loads.append(pltpu.make_async_copy(ref, states.at[pl.ds(i, 1)], state_load.at[i]))
+    for load in loads:
+        load.start()
+
     barrier = pltpu.get_barrier_semaphore()
     for partner in (low_partner, high_partner):
         pl.semaphore_signal(barrier, inc=1, device_id=(partner, shard), device_id_type=MESH)
@@ -188,18 +202,21 @@
         pl.semaphore_signal(barrier, inc=1, device_id=(rep, peer), device_id_type=MESH)
 
     span = LANES * GROUP
-
-    def squares(i, totals):
-        totals = list(totals)
-        for part in range(GROUP):
-            at = pl.ds(pl.multiple_of(i * span + part * LANES, LANES), LANES)
-            for j in range(steps):
-                grad = grad_ref[j // inner, j % inner, 0, :, at].astype(jnp.float32)
-                totals[j] = totals[j] + grad * grad
-        return tuple(totals)
-
     zero = jnp.zeros((8, LANES), jnp.float32)
-    totals = lax.fori_loop(0, columns // span, squares, (zero,) * steps)
+    totals = []
+    for t in range(outer):
+        loads[t].wait()
+
+        def squares(i, part_totals, t=t):
+            part_totals = list(part_totals)
+            for part in range(GROUP):
+                at = pl.ds(pl.multiple_of(i * span + part * LANES, LANES), LANES)
+                for k in range(inner):
+                    grad = grads[t, k, 0, :, at].astype(jnp.float32)
+                    part_totals[k] = part_totals[k] + grad * grad
+            return tuple(part_totals)
+
+        totals += lax.fori_loop(0, columns // span, squares, (zero,) * inner)
     lane = lax.broadcasted_iota(jnp.int32, (1, LANES), 1)
     share = jnp.zeros((1, LANES), jnp.float32)
     for j in range(steps):
@@ -240,7 +257,11 @@
         square_sum = square_sum + sums[offset]
     factor = clip_limit / jnp.maximum(jnp.sqrt(square_sum), clip_limit)
     for j in range(steps):
-        clips[j] = jnp.broadcast_to(factor[:, j : j + 1], (8, LANES))
+        clip = jnp.broadcast_to(factor[:, j : j + 1], (8, LANES))
+        gains[0, j] = (1.0 - beta_one) * clip
+        gains[1, j] = (1.0 - beta_two) * clip * clip
+    for load in loads[outer:]:
+        load.wait()
 
     keep = 1.0 - inner_rate * decay_rate
 
@@ -280,22 +301,22 @@
         firsts, seconds, moves = [], [], []
         spots = [pl.ds(pl.multiple_of(base + p * LANES, LANES), LANES) for p in range(GROUP)]
         for at in spots:
-            firsts.append(first_ref[0, :, at])
-            seconds.append(second_ref[0, :, at])
+            firsts.append(states[2, :, at])
+            seconds.append(states[3, :, at])
             moves.append([])
         for t in range(outer):
             move = [None] * GROUP
             for k in range(inner):
-                clip = clips[t * inner + k]
-                gain_one = (1.0 - beta_one) * clip
-                gain_two = (1.0 - beta_two) * clip * clip
+                gain_one = gains[0, t * inner + k]
+                gain_two = gains[1, t * inner + k]
                 for p, at in enumerate(spots):
-                    grad = grad_ref[t, k, 0, :, at].astype(jnp.float32)
+                    grad = grads[t, k, 0, :, at].astype(jnp.float32)
                     firsts[p] = beta_one * firsts[p] + gain_one * grad
                     seconds[p] = beta_two * seconds[p] + gain_two * (grad * grad)
                     floor = jnp.maximum(seconds[p], tiny)
                     bottom = floor * lax.rsqrt(floor) + adam_eps
-                    unit = firsts[p] / bottom
+                    guess = pl.reciprocal(bottom, approx=True)
+                    unit = firsts[p] * (guess * (2.0 - bottom * guess))
                     move[p] = unit if move[p] is None else keep * move[p] + unit
             for p in range(GROUP):
                 moves[p].append(inner_rate * move[p])
@@ -303,7 +324,7 @@
         for p, at in enumerate(spots):
             new_first_ref[0, :, at] = firsts[p]
             new_second_ref[0, :, at] = seconds[p]
-            values.append([slow_ref[0, :, at], momentum_ref[0, :, at]] + moves[p])
+            values.append([states[0, :, at], states[1, :, at]] + moves[p])
 
         def mixed(d):
             out = []
@@ -321,12 +342,13 @@
         def stored(target, out):
             for p in range(GROUP):
                 inside_at = pl.ds(pl.multiple_of(inside + p * LANES, LANES), LANES)
-                target[j, :, inside_at] = jnp.concatenate(out[p], axis=0).astype(jnp.bfloat16)
+                both = jnp.concatenate(out[p], axis=0)
+                target[j, :, inside_at] = both.astype(target.dtype)
 
         kind = j % 2
         stored(relay_out, mixed(3))
         stored(near_out, mixed(1 + kind))
-        stored(last_out, mixed(2 - kind))
+        stored(last_sum, mixed(2 - kind))
         for (slow, momentum), at in zip(mixed(0), spots):
             new_slow_ref[0, :, at] = slow
             new_momentum_ref[0, :, at] = momentum
@@ -339,33 +361,33 @@
 
         lax.fori_loop(0, width // span, body, 0)
         relay(j).start()
+        return carry
+
+    def first_stage_and_near(j, carry):
+        first_stage(j, carry)
         near(j).start()
         return carry
 
     def second_stage(j, carry):
         relay(j).wait_recv()
-        last_out[j] = (
-            last_out[j].astype(jnp.float32) + relay_in[j].astype(jnp.float32)
-        ).astype(jnp.bfloat16)
+        last_out[j] = (last_sum[j] + relay_in[j].astype(jnp.float32)).astype(jnp.bfloat16)
         last(j).start()
+        return carry
+
+    def near_stage(j, carry):
+        near(j).start()
         return carry
 
     def finish(j, carry):
         near(j).wait_recv()
         last(j).wait_recv()
-        at = pl.ds(pl.multiple_of(j * width, LANES), width)
-        arrived = near_in[j].astype(jnp.float32) + last_in[j].astype(jnp.float32)
-        new_slow_ref[0, :, at] += arrived[:8]
-        new_momentum_ref[0, :, at] += arrived[8:]
-        return carry
-
-    def both(j, carry):
-        first_stage(j, carry)
-        return second_stage(j - 2, carry)
-
-    lax.fori_loop(0, 2, first_stage, 0)
-    lax.fori_loop(2, pieces, both, 0)
-    lax.fori_loop(pieces - 2, pieces, second_stage, 0)
+        return carry
+
+    early = min(EARLY, pieces)
+    lax.fori_loop(0, early, first_stage_and_near, 0)
+    lax.fori_loop(early, pieces, first_stage, 0)
+    lax.fori_loop(0, pieces, second_stage, 0)
+    lax.fori_loop(early, pieces, near_stage, 0)
     lax.fori_loop(0, pieces, finish, 0)
 
     for copy in copies:
@@ -380,31 +402,73 @@
     lax.fori_loop(0, pieces, drained, 0)
 
 
+def finish_kernel(
+    slow_ref,
+    momentum_ref,
+    first_ref,
+    second_ref,
+    near_ref,
+    last_ref,
+    new_slow_ref,
+    new_momentum_ref,
+    new_first_ref,
+    new_second_ref,
+    slow,
+    momentum,
+    stored,
+):
+    pieces, rows, width = near_ref.shape
+    copies = [
+        pltpu.make_async_copy(first_ref, new_first_ref, stored.at[0]),
+        pltpu.make_async_copy(second_ref, new_second_ref, stored.at[1]),
+    ]
+    for copy in copies:
+        copy.start()
+
+    def add(j, carry):
+        at = pl.ds(pl.multiple_of(j * width, LANES), width)
+        arrived = near_ref[j].astype(jnp.float32) + last_ref[j].astype(jnp.float32)
+        slow[0, :, at] = slow_ref[0, :, at] + arrived[: rows // 2]
+        momentum[0, :, at] = momentum_ref[0, :, at] + arrived[rows // 2 :]
+        return carry
+
+    lax.fori_loop(0, pieces, add, 0)
+    for i, (value, target) in enumerate(((slow, new_slow_ref), (momentum, new_momentum_ref))):
+        copies.append(pltpu.make_async_copy(value, target, stored.at[2 + i]))
+        copies[-1].start()
+    for copy in copies:
+        copy.wait()
+
+
 def four_replicas(slow_weights, outer_momentum, adam_first, adam_second, gradients, pair_mask):
     shards = lax.axis_size("shard")
     outer, inner = gradients.shape[:2]
-    columns = slow_weights.shape[-1]
+    _, rows, columns = slow_weights.shape
     pieces = 2 * CHUNKS
-    width = columns // pieces
-    rows = 2 * slow_weights.shape[1]
-    piece = pltpu.VMEM((pieces, rows, width), jnp.bfloat16)
+    piece = (pieces, 2 * rows, columns // pieces)
+    half = pltpu.VMEM(piece, jnp.bfloat16)
     vmem = pl.BlockSpec(memory_space=pltpu.VMEM)
+    hbm = pl.BlockSpec(memory_space=pltpu.HBM)
     dma = pltpu.SemaphoreType.DMA
-    return pl.pallas_call(
+    slab = jax.ShapeDtypeStruct(slow_weights.shape, jnp.float32)
+    parts = pl.pallas_call(
         partial(kernel, shards),
-        out_shape=[jax.ShapeDtypeStruct(slow_weights.shape, jnp.float32)] * 4,
-        in_specs=[pl.BlockSpec(memory_space=pltpu.SMEM)] + [vmem] * 5,
-        out_specs=[vmem] * 4,
+        out_shape=[slab] * 4 + [jax.ShapeDtypeStruct(piece, jnp.bfloat16)] * 2,
+        in_specs=[pl.BlockSpec(memory_space=pltpu.SMEM)] + [hbm] * 5,
+        out_specs=[vmem] * 6,
         scratch_shapes=[
             pltpu.VMEM((8 * (outer + 2), 8, LANES), jnp.float32),
-            pltpu.VMEM((outer * inner, 8, LANES), jnp.float32),
+            pltpu.VMEM((2, outer * inner, 8, LANES), jnp.float32),
             pltpu.VMEM((shards, 1, LANES), jnp.float32),
-            piece,
-            piece,
-            piece,
-            piece,
-            piece,
-            piece,
+            pltpu.VMEM(gradients.shape, gradients.dtype),
+            pltpu.VMEM((4, rows, columns), jnp.float32),
+            half,
+            half,
+            pltpu.VMEM(piece, jnp.float32),
+            half,
+            half,
+            dma((outer,)),
+            dma((4,)),
             dma((shards,)),
             dma((shards,)),
             dma((pieces,)),
@@ -415,9 +479,21 @@
             dma((pieces,)),
         ],
         compiler_params=pltpu.CompilerParams(
-            collective_id=0, has_side_effects=True, vmem_limit_bytes=32 * 2**20
+            collective_id=0, has_side_effects=True, vmem_limit_bytes=54980608
         ),
     )(pair_mask, slow_weights, outer_momentum, adam_first, adam_second, gradients)
+    return pl.pallas_call(
+        finish_kernel,
+        out_shape=[slab] * 4,
+        in_specs=[vmem] * 6,
+        out_specs=[hbm] * 4,
+        scratch_shapes=[
+            pltpu.VMEM(slab.shape, jnp.float32),
+            pltpu.VMEM(slab.shape, jnp.float32),
+            dma((4,)),
+        ],
+        compiler_params=pltpu.CompilerParams(vmem_limit_bytes=16 * 2**20),
+    )(*parts)
 
 
 def on_device(*arguments):

time: 33.8 us -> 24.6 us (0.73)
  local copies, waits for them, and re-layouts: 8.85 us -> 0.65 us
  Pallas kernels: 24 us -> 23.2 us
    unnamed x16 -> x2, local copies, waits for them, and re-layouts: 8.85 us -> 0.65 us
    pallas_call x1 -> x2, Pallas kernels: 24 us -> 23.2 us  [the longest x1 22.2 us: four_replicas(): pl.pallas_call(partial(kernel, shards), out_shape=[slab] * 4 + [jax.Shape...]
where the time goes in v2:
time: 24.6 us; the launch traced here: 24.5 us
  Pallas kernels  23.2 us (94%)
  local copies, waits for them, and re-layouts  0.65 us (3%)
  between operations  0.65 us (3%)
    pallas_call x1, Pallas kernels, four_replicas(): pl.pallas_call(partial(kernel, shards), out_shape=[slab] * 4 + [jax.Shape...  22.2 us
    pallas_call x1, Pallas kernels, four_replicas(): pl.pallas_call(finish_kernel, out_shape=[slab] * 4, in_specs=[vmem] * 6,...  1 us
    unnamed x2, local copies, waits for them, and re-layouts  0.65 us

profile of v2, /device:TPU:0, one launch (start us, length us, event | category | flops | bytes accessed | tf_op | source)
XLA Modules:
  0.0 24.5 jit_solution(1491710263651007599)
XLA Ops:
  0.6 0.0 copy-start
  0.6 0.6 %copy-done = s32[4]{0:T(128)S(1)} copy-done((s32[4]{0:T(128)S(1)}, s32[4]{0:T(128)}, u32[]{:S(2)}) %copy-start) | copy-done | bytes 40
  1.3 22.2 %shard_map.93 = (f32[1,8,8192]{2,1,0:T(8,128)S(1)}, f32[1,8,8192]{2,1,0:T(8,128)S(1)}, f32[1,8,8192]{2,1,0:T(8,128)S(1)}, f32[1,8,8192]{2,1,0:T(8,128)S(1)}, bf1...) custom-call(s32[4]{0:T(128)S(1)} %copy-done, f32[1,8,8192]{2,1,0:T(8,128)} %slow_ref.1, ...), custom_call_target="tpu_custom_call" | custom-call | tf_op jit(solution)/shard_map/pallas_call | solution.py:454
  23.5 1.0 %shard_map.94 = (f32[1,8,8192]{2,1,0:T(8,128)}, f32[1,8,8192]{2,1,0:T(8,128)}, f32[1,8,8192]{2,1,0:T(8,128)}, f32[1,8,8192]{2,1,0:T(8,128)}) custom-call(f32[1,8,8192]{2,1,0:T(8,128)S(1)} %get-tuple-element.10.slow_ref, f32[1,8,8192]{2,1,0:T(8,128)S(1)} %get-tuple-element.11.momentum_ref, f32[1,8,8192]{2,1,0:T(8,128)S(1)} %get-tuple-element.12.first_ref, ...), custom_call_target="tpu_custom_call" | custom-call | tf_op jit(solution)/shard_map/pallas_call | solution.py:485
Async XLA Ops:
  0.6 0.7 %copy-start = (s32[4]{0:T(128)S(1)}, s32[4]{0:T(128)}, u32[]{:S(2)}) copy-start(s32[4]{0:T(128)} %mask_ref.1) | copy-start | bytes 52

commit v3 on v2

--- a/solution.py
+++ b/solution.py
@@ -271,7 +271,7 @@
             dst_ref=relay_in.at[j],
             send_sem=relay_send.at[j],
             recv_sem=relay_recv.at[j],
-            device_id=(low_partner + (j % 2) * (high_partner - low_partner), shard),
+            device_id=(low_partner + ((j + shard) % 2) * (high_partner - low_partner), shard),
             device_id_type=MESH,
         )
 
@@ -281,7 +281,7 @@
             dst_ref=near_in.at[j],
             send_sem=near_send.at[j],
             recv_sem=near_recv.at[j],
-            device_id=(low_partner + (j % 2) * (high_partner - low_partner), shard),
+            device_id=(low_partner + ((j + shard) % 2) * (high_partner - low_partner), shard),
             device_id_type=MESH,
         )
 
@@ -291,7 +291,7 @@
             dst_ref=last_in.at[j],
             send_sem=last_send.at[j],
             recv_sem=last_recv.at[j],
-            device_id=(high_partner - (j % 2) * (high_partner - low_partner), shard),
+            device_id=(high_partner - ((j + shard) % 2) * (high_partner - low_partner), shard),
             device_id_type=MESH,
         )
 
@@ -345,7 +345,7 @@
                 both = jnp.concatenate(out[p], axis=0)
                 target[j, :, inside_at] = both.astype(target.dtype)
 
-        kind = j % 2
+        kind = (j + shard) % 2
         stored(relay_out, mixed(3))
         stored(near_out, mixed(1 + kind))
         stored(last_sum, mixed(2 - kind))

time: 24.6 us -> 24.4 us (level)
  no operation moved by 1% of the time
where the time goes in v3:
time: 24.4 us; the launch traced here: 24.3 us
  Pallas kernels  23 us (94%)
  local copies, waits for them, and re-layouts  0.65 us (3%)
  between operations  0.65 us (3%)
    pallas_call x1, Pallas kernels, four_replicas(): pl.pallas_call(partial(kernel, shards), out_shape=[slab] * 4 + [jax.Shape...  22 us
    pallas_call x1, Pallas kernels, four_replicas(): pl.pallas_call(finish_kernel, out_shape=[slab] * 4, in_specs=[vmem] * 6,...  1 us
    unnamed x2, local copies, waits for them, and re-layouts  0.65 us

profile of v3, /device:TPU:0, one launch (start us, length us, event | category | flops | bytes accessed | tf_op | source)
XLA Modules:
  0.0 24.3 jit_solution(17179958337685040598)
XLA Ops:
  0.6 0.0 copy-start
  0.6 0.6 %copy-done = s32[4]{0:T(128)S(1)} copy-done((s32[4]{0:T(128)S(1)}, s32[4]{0:T(128)}, u32[]{:S(2)}) %copy-start) | copy-done | bytes 40
  1.3 22.0 %shard_map.93 = (f32[1,8,8192]{2,1,0:T(8,128)S(1)}, f32[1,8,8192]{2,1,0:T(8,128)S(1)}, f32[1,8,8192]{2,1,0:T(8,128)S(1)}, f32[1,8,8192]{2,1,0:T(8,128)S(1)}, bf1...) custom-call(s32[4]{0:T(128)S(1)} %copy-done, f32[1,8,8192]{2,1,0:T(8,128)} %slow_ref.1, ...), custom_call_target="tpu_custom_call" | custom-call | tf_op jit(solution)/shard_map/pallas_call | solution.py:454
  23.3 1.0 %shard_map.94 = (f32[1,8,8192]{2,1,0:T(8,128)}, f32[1,8,8192]{2,1,0:T(8,128)}, f32[1,8,8192]{2,1,0:T(8,128)}, f32[1,8,8192]{2,1,0:T(8,128)}) custom-call(f32[1,8,8192]{2,1,0:T(8,128)S(1)} %get-tuple-element.10.slow_ref, f32[1,8,8192]{2,1,0:T(8,128)S(1)} %get-tuple-element.11.momentum_ref, f32[1,8,8192]{2,1,0:T(8,128)S(1)} %get-tuple-element.12.first_ref, ...), custom_call_target="tpu_custom_call" | custom-call | tf_op jit(solution)/shard_map/pallas_call | solution.py:485
Async XLA Ops:
  0.6 0.7 %copy-start = (s32[4]{0:T(128)S(1)}, s32[4]{0:T(128)}, u32[]{:S(2)}) copy-start(s32[4]{0:T(128)} %mask_ref.1) | copy-start | bytes 52
